TPU v7x, 256 devices: a whole 4x4x8 slice. The times are simulated.
256 devices in a mesh: space: 32 (over x, z_lo, core), mode: 8 (over y, z_hi).
Axes of the slice: x: 4, y: 4, z: 8 (z_hi: 2, z_lo: 4; z = z_hi * 4 + z_lo), core: 2. Of those that a mesh axis runs over, the one named last changes fastest.
Arguments:
- field: float32 [56, 128, 48, 128], P('mode', 'space'), may hold values from -6 to 6
- coeff: float32 [6, 128, 48, 128], P(None, 'space'), may hold values from 0.02 to 0.4
- pairs: int32 [6, 168, 2], replicated, may hold values from 0 to 55
- values: float32 [6, 168], replicated, may hold values from -4 to 4
Outputs:
- first: float32 [56, 128, 48, 128], P('mode', 'space')
- second: float32 [56, 128, 48, 128], P('mode', 'space')
All inputs are finite; a program needn't handle non-finite values.
Results may differ from a plain program's by a relative error of at most 0.0001.
Values sent between devices are 32-bit elements; how exact they have to be, the bound alone decides.
A program may use at most 64 MiB of HBM per device.

v0:
```python
import functools

import jax
import jax.numpy as jnp
from jax import lax
from jax.experimental import pallas as pl
from jax.experimental.pallas import tpu as pltpu
from jax.sharding import PartitionSpec as P

MESH = pl.DeviceIdType.MESH
F32 = jnp.float32
BF16 = jnp.bfloat16

TERMS = 6
OWN = 7
SIDE = 28
MODES = 56
LAYERS = 4
ROWS = 12
CELLS = LAYERS * ROWS
FACES = 6
HIGH_ROWS = ROWS + 2
NR = 2
NC = ROWS // NR
AHEAD = 2


def kernel(
    field,
    coeff,
    pairs,
    values,
    first_out,
    second_out,
    U,
    F,
    S,
    XB1,
    XB2,
    YB1,
    YB2,
    A,
    FC,
    O1,
    O2,
    LF,
    L1,
    L2,
    y_send,
    y_recv,
    z_send,
    z_recv,
    c_send,
    c_recv,
    x_send,
    x_recv,
    b_send,
    b_recv,
    o_send,
    o_recv,
    loc,
    o_loc,
):
    space = lax.axis_index("space")
    mode = lax.axis_index("mode")
    y = mode // 2
    zhi = mode % 2

    def y_peer(step):
        return (space, lax.rem(y + step, 4) * 2 + zhi)

    partner = (space, y * 2 + 1 - zhi)

    def s_peer(step):
        return (space + step, mode)

    def send(src, dst, ss, rs, dev):
        return pltpu.make_async_remote_copy(
            src_ref=src, dst_ref=dst, send_sem=ss, recv_sem=rs, device_id=dev, device_id_type=MESH
        )

    def loop(n, body):
        def step(i, carry):
            body(i)
            return carry

        lax.fori_loop(0, n, step, 0)

    has_low = space > 0
    has_high = space < 31
    y_low = y > 0
    y_high = y < 3

    def chunk_row(at, c):
        return jnp.where(at % 2 == 0, c * NR, ROWS - (c + 1) * NR)

    U2 = U.reshape(NC * MODES * LAYERS * NR, 128)
    F2 = F.reshape(NC * MODES * LAYERS * NR, 128)
    S2 = S.reshape(NC * 32 * LAYERS * NR, 128)
    A2 = A.reshape(TERMS * 6 * HIGH_ROWS, 128)
    FC2 = FC.reshape(CELLS * 36, 128)

    A2[...] = jnp.zeros(A2.shape, F32)

    barrier = pltpu.get_barrier_semaphore()
    for step in (1, 2, 3):
        pl.semaphore_signal(barrier, inc=1, device_id=y_peer(step), device_id_type=MESH)
    pl.semaphore_signal(barrier, inc=1, device_id=partner, device_id_type=MESH)

    @pl.when(has_low)
    def _():
        pl.semaphore_signal(barrier, inc=1, device_id=s_peer(-1), device_id_type=MESH)

    @pl.when(has_high)
    def _():
        pl.semaphore_signal(barrier, inc=1, device_id=s_peer(1), device_id_type=MESH)

    pl.semaphore_wait(barrier, 4 + has_low.astype(jnp.int32) + has_high.astype(jnp.int32))

    def y_copy(step, c):
        to = lax.rem(y + step, 4)
        return send(
            field.at[:, :, pl.ds(to * ROWS + chunk_row(to, c), NR)],
            U.at[c, pl.ds(zhi * SIDE + y * OWN, OWN)],
            y_send.at[step, c],
            y_recv.at[step, c],
            y_peer(step),
        )

    def y_arrival(step, c):
        src = lax.rem(y + 4 - step, 4)
        return send(
            field.at[:, :, pl.ds(0, NR)],
            U.at[c, pl.ds(zhi * SIDE + src * OWN, OWN)],
            y_send.at[step, c],
            y_recv.at[step, c],
            y_peer(step),
        )

    def own_rows(c):
        return field.at[:, :, pl.ds(y * ROWS + chunk_row(y, c), NR)]

    def z_copy(c, j):
        at = pl.ds(zhi * SIDE + lax.rem(y + j, 4) * OWN, OWN)
        src = own_rows(c) if j == 0 else U.at[c, at]
        return send(src, U.at[c, at], z_send.at[c, j], z_recv.at[c, j], partner)

    def z_arrival(c, j):
        at = pl.ds((1 - zhi) * SIDE + lax.rem(y + j, 4) * OWN, OWN)
        return send(U.at[c, at], U.at[c, at], z_send.at[c, j], z_recv.at[c, j], partner)

    for c in range(AHEAD):
        z_copy(c, 0).start()

    def start_y(c):
        for step in (1, 3, 2):
            y_copy(step, c).start()

    loop(NC, start_y)

    def own_copy(c):
        return pltpu.make_async_copy(own_rows(c), U.at[c, pl.ds(zhi * SIDE + y * OWN, OWN)], loc.at[3 + c])

    loop(NC, lambda c: own_copy(c).start())

    own_a = pltpu.make_async_copy(
        coeff.at[:, :, pl.ds(y * ROWS, ROWS)], A.at[:, pl.ds(1, LAYERS), pl.ds(1, ROWS)], loc.at[0]
    )
    low_a = pltpu.make_async_copy(
        coeff.at[:, :, pl.ds(jnp.maximum(y * ROWS - 1, 0), 1)],
        A.at[:, pl.ds(1, LAYERS), pl.ds(0, 1)],
        loc.at[1],
    )
    high_a = pltpu.make_async_copy(
        coeff.at[:, :, pl.ds(jnp.minimum(y * ROWS + ROWS, 47), 1)],
        A.at[:, pl.ds(1, LAYERS), pl.ds(ROWS + 1, 1)],
        loc.at[2],
    )

    def a_copy(up):
        l, slot, s = (LAYERS - 1, 0, 1) if up else (0, LAYERS + 1, -1)
        return send(
            coeff.at[:, l, pl.ds(y * ROWS, ROWS)],
            A.at[:, slot, pl.ds(1, ROWS)],
            c_send.at[int(up)],
            c_recv.at[int(up)],
            s_peer(s),
        )

    own_a.start()
    pl.when(y_low)(low_a.start)
    pl.when(y_high)(high_a.start)
    pl.when(has_high)(a_copy(True).start)
    pl.when(has_low)(a_copy(False).start)

    def y_to_z(c):
        for j in (1, 3, 2):
            y_arrival(4 - j, c).wait_recv()
            z_copy(c, j).start()

    for c in range(AHEAD):
        y_to_z(c)

    def mode_id(at):
        side = (at >= SIDE).astype(jnp.int32)
        rest = at - SIDE * side
        block = sum((rest >= OWN * n).astype(jnp.int32) for n in (1, 2, 3))
        return rest + OWN * block + OWN * side

    nnz = values.shape[1]
    eye = lax.broadcasted_iota(jnp.int32, (nnz, nnz), 0) == lax.broadcasted_iota(jnp.int32, (nnz, nnz), 1)
    slot = lax.broadcasted_iota(jnp.int32, (nnz, 256), 1) % 64
    col_id = jnp.where(slot < MODES, mode_id(slot), -1)
    low_part = lax.broadcasted_iota(jnp.int32, (8, 256), 1) >= 128

    def build(tiles, start, count, target):
        at = lax.broadcasted_iota(jnp.int32, (tiles * 8, nnz), 0)
        ids = jnp.where(at < count, mode_id(at + start), -1)

        def term(k):
            both = pairs[k]
            cols = jnp.sum(jnp.where(eye, both[1:2, :], 0), axis=1, keepdims=True)
            left = jnp.where(ids == both[0:1, :], values[pl.ds(k, 1), :], 0.0)
            right = jnp.where(col_id == cols, 1.0, 0.0)
            full = jnp.dot(left, right, precision=lax.Precision.HIGHEST, preferred_element_type=F32)
            for t in range(tiles):
                part = full[t * 8 : t * 8 + 8]
                high = part.astype(BF16).astype(F32)
                LF[pl.ds(pl.multiple_of(t * 48 + k * 8, 8), 8), :] = jnp.where(low_part, part - high, high)

        loop(TERMS, term)
        target[...] = LF[0 : tiles * 48, :].astype(BF16)

    build(7, 0, MODES, L1)
    build(4, zhi * SIDE, SIDE, L2)

    own_a.wait()
    pl.when(y_low)(low_a.wait)
    pl.when(y_high)(high_a.wait)
    pl.when(has_low)(a_copy(True).wait_recv)
    pl.when(has_high)(a_copy(False).wait_recv)
    lanes = lax.broadcasted_iota(jnp.int32, (ROWS, 128), 1)

    def faces(i):
        k = i // LAYERS
        l = lax.rem(i, LAYERS)
        base = (k * 6 + l + 1) * HIGH_ROWS + 1
        a = A2[pl.ds(base, ROWS), :]
        near = (
            A2[pl.ds(base - HIGH_ROWS, ROWS), :],
            A2[pl.ds(base + HIGH_ROWS, ROWS), :],
            A2[pl.ds(base - 1, ROWS), :],
            A2[pl.ds(base + 1, ROWS), :],
            jnp.where(lanes == 0, 0.0, pltpu.roll(a, 1, 1)),
            jnp.where(lanes == 127, 0.0, pltpu.roll(a, 127, 1)),
        )
        for d in range(FACES):
            FC2[pl.ds(l * (ROWS * 36) + d * 6 + k, ROWS, stride=36), :] = 0.5 * (a + near[d])

    loop(TERMS * LAYERS, faces)

    def clear(i):
        l = i // HIGH_ROWS
        r = lax.rem(i, HIGH_ROWS)
        O1[l, r] = jnp.zeros((MODES, 128), F32)
        O2[l, r] = jnp.zeros((32, 128), F32)

    loop(6 * HIGH_ROWS, clear)
    loop(NC, lambda c: own_copy(c).wait())

    def mix(matrix, a, b):
        u = jnp.concatenate([a, b], axis=1)
        u = jnp.concatenate([u, jnp.zeros((8, 256), F32)], axis=0)
        high = u.astype(BF16)
        low = (u - high.astype(F32)).astype(BF16)
        return jnp.dot(
            matrix[...], jnp.concatenate([high, low, high, low], axis=0), preferred_element_type=F32
        )

    def face_sum(row, d, v):
        total = None
        for k in range(TERMS):
            term = FC2[pl.ds(row * 36 + d * 6 + k, 1), :] * v[k]
            total = term if total is None else total + term
        return total

    lane8 = lax.broadcasted_iota(jnp.int32, (8, 128), 1)

    def apply_chunk(src, O, matrix, tiles, c):
        def pair(p):
            i = p // 2
            l = 2 * lax.rem(p, 2)
            r = chunk_row(y, c) + i
            base = c * (MODES * LAYERS * NR) + l * NR + i
            full = mix(
                matrix,
                src[pl.ds(base, MODES, stride=LAYERS * NR), :],
                src[pl.ds(base + NR, MODES, stride=LAYERS * NR), :],
            )
            for h in range(2):
                at_l, at_r, row = l + 1 + h, r + 1, (l + h) * ROWS + r
                for t in range(tiles):
                    v = [full[t * 48 + k * 8 : t * 48 + k * 8 + 8, h * 128 : h * 128 + 128] for k in range(TERMS)]
                    xl, xr, yl, yr, zl, zr = [face_sum(row, d, v) for d in range(FACES)]
                    zl_moved = jnp.where(lane8 == 127, 0.0, pltpu.roll(zl, 127, 1))
                    zr_moved = jnp.where(lane8 == 0, 0.0, pltpu.roll(zr, 1, 1))
                    tile = pl.ds(t * 8, 8)
                    O[at_l, at_r, tile, :] += (xl + xr) + (yl + yr) + ((zl + zr) - (zl_moved + zr_moved))
                    O[at_l - 1, at_r, tile, :] -= xl
                    O[at_l + 1, at_r, tile, :] -= xr
                    O[at_l, at_r - 1, tile, :] -= yl
                    O[at_l, at_r + 1, tile, :] -= yr

        loop(2 * NR, pair)

    def borders(n):
        O, XB, YB, count = ((O1, XB1, YB1, MODES), (O2, XB2, YB2, SIDE))[n]
        some = pl.ds(0, count)

        def x(up, c):
            l, slot, s = (LAYERS + 1, 0, 1) if up else (0, 1, -1)
            return send(
                O.at[l, pl.ds(chunk_row(y, c) + 1, NR), some],
                XB.at[slot, c, :, some],
                x_send.at[n, int(up), c],
                x_recv.at[n, int(up), c],
                s_peer(s),
            )

        def yy(up):
            r, slot, s = (ROWS + 1, 0, 1) if up else (0, 1, 3)
            return send(
                O.at[pl.ds(1, LAYERS), r, some],
                YB.at[slot, :, some],
                b_send.at[n, int(up)],
                b_recv.at[n, int(up)],
                y_peer(s),
            )

        return x, yy

    def early_up(c):
        return jnp.where(y % 2 == 0, c == NC - 1, c == 0)

    def early_down(c):
        return jnp.where(y % 2 == 0, c == 0, c == NC - 1)

    def send_borders(n, c):
        x, yy = borders(n)
        pl.when(has_high)(x(True, c).start)
        pl.when(has_low)(x(False, c).start)
        pl.when(jnp.logical_and(y_high, early_up(c)))(yy(True).start)
        pl.when(jnp.logical_and(y_low, early_down(c)))(yy(False).start)

    def add_borders(n, c):
        x, yy = borders(n)
        O, XB, YB, modes = ((O1, XB1, YB1, MODES), (O2, XB2, YB2, 32))[n]
        r = chunk_row(y, c) + 1

        @pl.when(has_low)
        def _():
            x(True, c).wait_recv()
            for i in range(NR):
                O[1, r + i] += XB[0, c, i]

        @pl.when(has_high)
        def _():
            x(False, c).wait_recv()
            for i in range(NR):
                O[LAYERS, r + i] += XB[1, c, i]

        @pl.when(jnp.logical_and(y_low, early_down(c)))
        def _():
            yy(True).wait_recv()
            for l in range(LAYERS):
                O[l + 1, 1] += YB[0, l]

        @pl.when(jnp.logical_and(y_high, early_up(c)))
        def _():
            yy(False).wait_recv()
            for l in range(LAYERS):
                O[l + 1, ROWS] += YB[1, l]

    def out_copy(n, step, c):
        to = lax.rem(y + step, 4)
        if n == 0:
            src, dst = F.at[c, pl.ds(zhi * SIDE + to * OWN, OWN)], first_out
        else:
            src, dst = S.at[c, pl.ds(to * OWN, OWN)], second_out
        dst = dst.at[:, :, pl.ds(y * ROWS + chunk_row(y, c), NR)]
        if step == 0:
            return pltpu.make_async_copy(src, dst, o_loc.at[n, c])
        return send(src, dst, o_send.at[n, step, c], o_recv.at[n, step, c], y_peer(step))

    def out_arrival(n, step, c):
        src = lax.rem(y + 4 - step, 4)
        dst = (first_out, second_out)[n].at[:, :, pl.ds(src * ROWS + chunk_row(src, c), NR)]
        return send(F.at[0, pl.ds(0, OWN)], dst, o_send.at[n, step, c], o_recv.at[n, step, c], y_peer(step))

    def finish(n, c):
        add_borders(n, c)
        O, to, modes = ((O1, F2, MODES), (O2, S2, 32))[n]
        r = chunk_row(y, c) + 1
        for i in range(NR):
            for l in range(LAYERS):
                to[pl.ds(c * (modes * LAYERS * NR) + l * NR + i, modes, stride=LAYERS * NR), :] = O[l + 1, r + i]
        for step in (2, 1, 3, 0):
            out_copy(n, step, c).start()

    def stage(c):
        @pl.when(c < NC)
        def _():
            for j in range(4):
                z_arrival(c, j).wait_recv()
            apply_chunk(U2, O1, L1, 7, c)
            send_borders(0, c)

        @pl.when(c + AHEAD < NC)
        def _():
            z_copy(c + AHEAD, 0).start()
            y_to_z(c + AHEAD)

        @pl.when(jnp.logical_and(c >= 1, c <= NC))
        def _():
            finish(0, c - 1)
            apply_chunk(F2, O2, L2, 4, c - 1)
            send_borders(1, c - 1)

        @pl.when(c >= 2)
        def _():
            finish(1, c - 2)

    loop(NC + 2, stage)

    def drain(c):
        for step in (1, 2, 3):
            y_copy(step, c).wait_send()
        for j in range(4):
            z_copy(c, j).wait_send()
        for n in range(2):
            x, _ = borders(n)
            pl.when(has_high)(x(True, c).wait_send)
            pl.when(has_low)(x(False, c).wait_send)
            out_copy(n, 0, c).wait()
            for step in (1, 2, 3):
                out_copy(n, step, c).wait_send()
                out_arrival(n, step, c).wait_recv()

    loop(NC, drain)
    for n in range(2):
        _, yy = borders(n)
        pl.when(y_high)(yy(True).wait_send)
        pl.when(y_low)(yy(False).wait_send)
    pl.when(has_high)(a_copy(True).wait_send)
    pl.when(has_low)(a_copy(False).wait_send)


def per_device(field, coeff, pairs, values):
    vmem = pl.BlockSpec(memory_space=pltpu.VMEM)
    hbm = pl.BlockSpec(memory_space=pl.ANY)
    out = jax.ShapeDtypeStruct((OWN, LAYERS, 48, 1, 128), F32)
    sem = pltpu.SemaphoreType.DMA
    first, second = pl.pallas_call(
        kernel,
        out_shape=(out, out),
        in_specs=[hbm, hbm, vmem, vmem],
        out_specs=(vmem, vmem),
        scratch_shapes=[
            pltpu.VMEM((NC, MODES, LAYERS, NR, 1, 128), F32),
            pltpu.VMEM((NC, MODES, LAYERS, NR, 1, 128), F32),
            pltpu.VMEM((NC, 32, LAYERS, NR, 1, 128), F32),
            pltpu.VMEM((2, NC, NR, MODES, 128), F32),
            pltpu.VMEM((2, NC, NR, 32, 128), F32),
            pltpu.VMEM((2, LAYERS, MODES, 128), F32),
            pltpu.VMEM((2, LAYERS, 32, 128), F32),
            pltpu.VMEM((TERMS, 6, HIGH_ROWS, 1, 128), F32),
            pltpu.VMEM((CELLS * 36, 1, 128), F32),
            pltpu.VMEM((6, HIGH_ROWS, MODES, 128), F32),
            pltpu.VMEM((6, HIGH_ROWS, 32, 128), F32),
            pltpu.VMEM((336, 256), F32),
            pltpu.VMEM((336, 256), BF16),
            pltpu.VMEM((192, 256), BF16),
            sem((4, NC)),
            sem((4, NC)),
            sem((NC, 4)),
            sem((NC, 4)),
            sem((2,)),
            sem((2,)),
            sem((2, 2, NC)),
            sem((2, 2, NC)),
            sem((2, 2)),
            sem((2, 2)),
            sem((2, 4, NC)),
            sem((2, 4, NC)),
            sem((3 + NC,)),
            sem((2, NC)),
        ],
        compiler_params=pltpu.CompilerParams(
            collective_id=0, has_side_effects=True, vmem_limit_bytes=48 << 20
        ),
    )(
        field.reshape(OWN, LAYERS, 48, 1, 128),
        coeff.reshape(TERMS, LAYERS, 48, 1, 128),
        jnp.transpose(pairs, (0, 2, 1)),
        values,
    )
    return first.reshape(field.shape), second.reshape(field.shape)


def solution(mesh):
    in_specs = (P("mode", "space", None, None), P(None, "space", None, None), P(), P())
    out_specs = (P("mode", "space", None, None), P("mode", "space", None, None))
    return jax.shard_map(
        per_device, mesh=mesh, in_specs=in_specs, out_specs=out_specs, check_vma=False
    )
```

profile of v0, /device:TPU:6, one launch (start us, length us, event | category | flops | bytes accessed | tf_op | source)
XLA Modules:
  0.0 74.3 jit_solution(16928218651777906976)
XLA Ops:
  0.6 0.0 copy-start
  0.6 1.1 %copy-done = f32[7,4,48,128]{3,2,1,0:T(8,128)S(1)} copy-done((f32[7,4,48,128]{3,2,1,0:T(8,128)S(1)}, f32[7,4,48,128]{3,2,1,0:T(8,128)}, u32[]{:S(2)}) %copy-start) | copy-done | bytes 688152
  1.7 0.0 copy-start.1
  1.7 1.1 %copy-done.1 = f32[6,4,48,128]{3,2,1,0:T(8,128)S(1)} copy-done((f32[6,4,48,128]{3,2,1,0:T(8,128)S(1)}, f32[6,4,48,128]{3,2,1,0:T(8,128)}, u32[]{:S(2)}) %copy-start.1) | copy-done | bytes 589848
  2.8 0.0 copy-start.2
  2.8 0.7 copy-done.2
  3.5 0.0 copy-start.3
  3.5 0.7 copy-done.3
  4.2 68.4 %shard_map.59 = (f32[7,4,48,1,128]{4,3,2,1,0:T(1,128)S(1)}, f32[7,4,48,1,128]{4,3,2,1,0:T(1,128)S(1)}) custom-call(f32[7,4,48,1,128]{4,3,2,1,0:T(1,128)S(1)} %bitcast.5, f32[6,4,48,1,128]{4,3,2,1,0:T(1,128)S(1)} %bitcast.8, s32[6,2,168]{2,1,0:T(2,128)S(1)} %bitcast.9, f32[6,168]{1,0:T(8,128)S(1)} %copy-done.3), custom_call_target="tpu_custom_call" | custom-call | tf_op jit(solution)/shard_map/pallas_call | solution.py:463
  72.6 0.8 %copy.8 = f32[7,4,48,128]{3,2,1,0:T(8,128)} copy(f32[7,4,48,128]{3,2,1,0:T(8,128)S(1)} %bitcast.7) | data formatting | bytes 1376256
  73.4 0.8 %copy.9 = f32[7,4,48,128]{3,2,1,0:T(8,128)} copy(f32[7,4,48,128]{3,2,1,0:T(8,128)S(1)} %bitcast.6) | data formatting | bytes 1376256
Async XLA Ops:
  0.6 1.1 %copy-start = (f32[7,4,48,128]{3,2,1,0:T(8,128)S(1)}, f32[7,4,48,128]{3,2,1,0:T(8,128)}, u32[]{:S(2)}) copy-start(f32[7,4,48,128]{3,2,1,0:T(8,128)} %param.4) | copy-start | bytes 2064388
  1.7 1.1 %copy-start.1 = (f32[6,4,48,128]{3,2,1,0:T(8,128)S(1)}, f32[6,4,48,128]{3,2,1,0:T(8,128)}, u32[]{:S(2)}) copy-start(f32[6,4,48,128]{3,2,1,0:T(8,128)} %param.5) | copy-start | bytes 1769476
  2.8 0.7 copy-start.2
  3.5 0.7 copy-start.3
where the time goes:
time: 74.6 us; the launch traced here: 74.3 us
  Pallas kernels  68.4 us (92%)
  local copies, waits for them, and re-layouts  5.26 us (7%)
    pallas_call x1, Pallas kernels, per_device(): pl.pallas_call(kernel, out_shape=(out, out), in_specs=[hbm, hbm, vmem, vm...  68.4 us
    unnamed x10, local copies, waits for them, and re-layouts  5.26 us

commit v1 on v0

--- a/solution.py
+++ b/solution.py
@@ -22,7 +22,8 @@
 HIGH_ROWS = ROWS + 2
 NR = 2
 NC = ROWS // NR
-AHEAD = 2
+AHEAD = 3
+LAG = 2
 
 
 def kernel(
@@ -74,6 +75,11 @@
     def s_peer(step):
         return (space + step, mode)
 
+    at_end = {1: space % 8 == 7, -1: space % 8 == 0}
+
+    def near_peer(step):
+        return (space + step, jnp.where(at_end[step], y * 2 + 1 - zhi, mode))
+
     def send(src, dst, ss, rs, dev):
         return pltpu.make_async_remote_copy(
             src_ref=src, dst_ref=dst, send_sem=ss, recv_sem=rs, device_id=dev, device_id_type=MESH
@@ -91,8 +97,8 @@
     y_low = y > 0
     y_high = y < 3
 
-    def chunk_row(at, c):
-        return jnp.where(at % 2 == 0, c * NR, ROWS - (c + 1) * NR)
+    def chunk_row(c):
+        return NR * jnp.where(c % 2 == 0, c // 2, NC - 1 - c // 2)
 
     U2 = U.reshape(NC * MODES * LAYERS * NR, 128)
     F2 = F.reshape(NC * MODES * LAYERS * NR, 128)
@@ -107,61 +113,56 @@
         pl.semaphore_signal(barrier, inc=1, device_id=y_peer(step), device_id_type=MESH)
     pl.semaphore_signal(barrier, inc=1, device_id=partner, device_id_type=MESH)
 
-    @pl.when(has_low)
-    def _():
-        pl.semaphore_signal(barrier, inc=1, device_id=s_peer(-1), device_id_type=MESH)
-
-    @pl.when(has_high)
-    def _():
-        pl.semaphore_signal(barrier, inc=1, device_id=s_peer(1), device_id_type=MESH)
-
-    pl.semaphore_wait(barrier, 4 + has_low.astype(jnp.int32) + has_high.astype(jnp.int32))
+    expected = jnp.int32(4)
+    for present, step in ((has_low, -1), (has_high, 1)):
+        turned = jnp.logical_and(present, at_end[step])
+
+        @pl.when(present)
+        def _(step=step):
+            pl.semaphore_signal(barrier, inc=1, device_id=s_peer(step), device_id_type=MESH)
+
+        @pl.when(turned)
+        def _(step=step):
+            pl.semaphore_signal(barrier, inc=1, device_id=near_peer(step), device_id_type=MESH)
+
+        expected = expected + present.astype(jnp.int32) + turned.astype(jnp.int32)
+    pl.semaphore_wait(barrier, expected)
 
     def y_copy(step, c):
         to = lax.rem(y + step, 4)
         return send(
-            field.at[:, :, pl.ds(to * ROWS + chunk_row(to, c), NR)],
+            field.at[:, :, pl.ds(to * ROWS + chunk_row(c), NR)],
             U.at[c, pl.ds(zhi * SIDE + y * OWN, OWN)],
-            y_send.at[step, c],
-            y_recv.at[step, c],
+            y_send.at[0],
+            y_recv.at[c],
             y_peer(step),
         )
 
-    def y_arrival(step, c):
-        src = lax.rem(y + 4 - step, 4)
-        return send(
-            field.at[:, :, pl.ds(0, NR)],
-            U.at[c, pl.ds(zhi * SIDE + src * OWN, OWN)],
-            y_send.at[step, c],
-            y_recv.at[step, c],
-            y_peer(step),
-        )
+    def wait_y(c):
+        three = U.at[c, pl.ds(0, 3 * OWN)]
+        send(three, three, y_send.at[0], y_recv.at[c], partner).wait_recv()
 
     def own_rows(c):
-        return field.at[:, :, pl.ds(y * ROWS + chunk_row(y, c), NR)]
+        return field.at[:, :, pl.ds(y * ROWS + chunk_row(c), NR)]
 
     def z_copy(c, j):
         at = pl.ds(zhi * SIDE + lax.rem(y + j, 4) * OWN, OWN)
         src = own_rows(c) if j == 0 else U.at[c, at]
-        return send(src, U.at[c, at], z_send.at[c, j], z_recv.at[c, j], partner)
-
-    def z_arrival(c, j):
-        at = pl.ds((1 - zhi) * SIDE + lax.rem(y + j, 4) * OWN, OWN)
-        return send(U.at[c, at], U.at[c, at], z_send.at[c, j], z_recv.at[c, j], partner)
-
-    for c in range(AHEAD):
-        z_copy(c, 0).start()
-
-    def start_y(c):
+        return send(src, U.at[c, at], z_send.at[0], z_recv.at[c], partner)
+
+    def wait_z(c):
+        side = U.at[c, pl.ds((1 - zhi) * SIDE, SIDE)]
+        send(side, side, z_send.at[0], z_recv.at[c], partner).wait_recv()
+
+    def own_copy(c):
+        return pltpu.make_async_copy(own_rows(c), U.at[c, pl.ds(zhi * SIDE + y * OWN, OWN)], loc.at[3])
+
+    def start_field(c):
         for step in (1, 3, 2):
             y_copy(step, c).start()
-
-    loop(NC, start_y)
-
-    def own_copy(c):
-        return pltpu.make_async_copy(own_rows(c), U.at[c, pl.ds(zhi * SIDE + y * OWN, OWN)], loc.at[3 + c])
-
-    loop(NC, lambda c: own_copy(c).start())
+        z_copy(c, 0).start()
+
+    loop(NC, start_field)
 
     own_a = pltpu.make_async_copy(
         coeff.at[:, :, pl.ds(y * ROWS, ROWS)], A.at[:, pl.ds(1, LAYERS), pl.ds(1, ROWS)], loc.at[0]
@@ -184,7 +185,7 @@
             A.at[:, slot, pl.ds(1, ROWS)],
             c_send.at[int(up)],
             c_recv.at[int(up)],
-            s_peer(s),
+            near_peer(s),
         )
 
     own_a.start()
@@ -193,13 +194,14 @@
     pl.when(has_high)(a_copy(True).start)
     pl.when(has_low)(a_copy(False).start)
 
+    loop(NC, lambda c: own_copy(c).start())
+
     def y_to_z(c):
-        for j in (1, 3, 2):
-            y_arrival(4 - j, c).wait_recv()
+        wait_y(c)
+        for j in (1, 2, 3):
             z_copy(c, j).start()
 
-    for c in range(AHEAD):
-        y_to_z(c)
+    loop(AHEAD, y_to_z)
 
     def mode_id(at):
         side = (at >= SIDE).astype(jnp.int32)
@@ -266,7 +268,8 @@
         O2[l, r] = jnp.zeros((32, 128), F32)
 
     loop(6 * HIGH_ROWS, clear)
-    loop(NC, lambda c: own_copy(c).wait())
+    own = U.at[:, pl.ds(0, OWN)]
+    pltpu.make_async_copy(own, own, loc.at[3]).wait()
 
     def mix(matrix, a, b):
         u = jnp.concatenate([a, b], axis=1)
@@ -290,7 +293,7 @@
         def pair(p):
             i = p // 2
             l = 2 * lax.rem(p, 2)
-            r = chunk_row(y, c) + i
+            r = chunk_row(c) + i
             base = c * (MODES * LAYERS * NR) + l * NR + i
             full = mix(
                 matrix,
@@ -320,11 +323,11 @@
         def x(up, c):
             l, slot, s = (LAYERS + 1, 0, 1) if up else (0, 1, -1)
             return send(
-                O.at[l, pl.ds(chunk_row(y, c) + 1, NR), some],
+                O.at[l, pl.ds(chunk_row(c) + 1, NR), some],
                 XB.at[slot, c, :, some],
-                x_send.at[n, int(up), c],
+                x_send.at[n, int(up)],
                 x_recv.at[n, int(up), c],
-                s_peer(s),
+                (near_peer, s_peer)[n](s),
             )
 
         def yy(up):
@@ -339,23 +342,23 @@
 
         return x, yy
 
-    def early_up(c):
-        return jnp.where(y % 2 == 0, c == NC - 1, c == 0)
-
-    def early_down(c):
-        return jnp.where(y % 2 == 0, c == 0, c == NC - 1)
+    def is_top(c):
+        return c == 1
+
+    def is_bottom(c):
+        return c == 0
 
     def send_borders(n, c):
         x, yy = borders(n)
         pl.when(has_high)(x(True, c).start)
         pl.when(has_low)(x(False, c).start)
-        pl.when(jnp.logical_and(y_high, early_up(c)))(yy(True).start)
-        pl.when(jnp.logical_and(y_low, early_down(c)))(yy(False).start)
+        pl.when(jnp.logical_and(y_high, is_top(c)))(yy(True).start)
+        pl.when(jnp.logical_and(y_low, is_bottom(c)))(yy(False).start)
 
     def add_borders(n, c):
         x, yy = borders(n)
         O, XB, YB, modes = ((O1, XB1, YB1, MODES), (O2, XB2, YB2, 32))[n]
-        r = chunk_row(y, c) + 1
+        r = chunk_row(c) + 1
 
         @pl.when(has_low)
         def _():
@@ -369,13 +372,13 @@
             for i in range(NR):
                 O[LAYERS, r + i] += XB[1, c, i]
 
-        @pl.when(jnp.logical_and(y_low, early_down(c)))
+        @pl.when(jnp.logical_and(y_low, is_bottom(c)))
         def _():
             yy(True).wait_recv()
             for l in range(LAYERS):
                 O[l + 1, 1] += YB[0, l]
 
-        @pl.when(jnp.logical_and(y_high, early_up(c)))
+        @pl.when(jnp.logical_and(y_high, is_top(c)))
         def _():
             yy(False).wait_recv()
             for l in range(LAYERS):
@@ -387,20 +390,15 @@
             src, dst = F.at[c, pl.ds(zhi * SIDE + to * OWN, OWN)], first_out
         else:
             src, dst = S.at[c, pl.ds(to * OWN, OWN)], second_out
-        dst = dst.at[:, :, pl.ds(y * ROWS + chunk_row(y, c), NR)]
+        dst = dst.at[:, :, pl.ds(y * ROWS + chunk_row(c), NR)]
         if step == 0:
-            return pltpu.make_async_copy(src, dst, o_loc.at[n, c])
-        return send(src, dst, o_send.at[n, step, c], o_recv.at[n, step, c], y_peer(step))
-
-    def out_arrival(n, step, c):
-        src = lax.rem(y + 4 - step, 4)
-        dst = (first_out, second_out)[n].at[:, :, pl.ds(src * ROWS + chunk_row(src, c), NR)]
-        return send(F.at[0, pl.ds(0, OWN)], dst, o_send.at[n, step, c], o_recv.at[n, step, c], y_peer(step))
+            return pltpu.make_async_copy(src, dst, o_loc.at[n])
+        return send(src, dst, o_send.at[n], o_recv.at[n], y_peer(step))
 
     def finish(n, c):
         add_borders(n, c)
         O, to, modes = ((O1, F2, MODES), (O2, S2, 32))[n]
-        r = chunk_row(y, c) + 1
+        r = chunk_row(c) + 1
         for i in range(NR):
             for l in range(LAYERS):
                 to[pl.ds(c * (modes * LAYERS * NR) + l * NR + i, modes, stride=LAYERS * NR), :] = O[l + 1, r + i]
@@ -410,49 +408,45 @@
     def stage(c):
         @pl.when(c < NC)
         def _():
-            for j in range(4):
-                z_arrival(c, j).wait_recv()
+            wait_z(c)
             apply_chunk(U2, O1, L1, 7, c)
             send_borders(0, c)
 
         @pl.when(c + AHEAD < NC)
         def _():
-            z_copy(c + AHEAD, 0).start()
             y_to_z(c + AHEAD)
 
-        @pl.when(jnp.logical_and(c >= 1, c <= NC))
-        def _():
-            finish(0, c - 1)
-            apply_chunk(F2, O2, L2, 4, c - 1)
-            send_borders(1, c - 1)
-
-        @pl.when(c >= 2)
-        def _():
-            finish(1, c - 2)
-
-    loop(NC + 2, stage)
-
-    def drain(c):
-        for step in (1, 2, 3):
-            y_copy(step, c).wait_send()
-        for j in range(4):
-            z_copy(c, j).wait_send()
-        for n in range(2):
-            x, _ = borders(n)
-            pl.when(has_high)(x(True, c).wait_send)
-            pl.when(has_low)(x(False, c).wait_send)
-            out_copy(n, 0, c).wait()
-            for step in (1, 2, 3):
-                out_copy(n, step, c).wait_send()
-                out_arrival(n, step, c).wait_recv()
-
-    loop(NC, drain)
+        @pl.when(jnp.logical_and(c >= LAG, c < NC + LAG))
+        def _():
+            finish(0, c - LAG)
+            apply_chunk(F2, O2, L2, 4, c - LAG)
+            send_borders(1, c - LAG)
+
+        @pl.when(c >= 2 * LAG)
+        def _():
+            finish(1, c - 2 * LAG)
+
+    loop(NC + 2 * LAG, stage)
+
+    three = U.at[:, pl.ds(0, 3 * OWN)]
+    side = U.at[:, pl.ds(0, SIDE)]
+    send(three, three, y_send.at[0], y_recv.at[0], partner).wait_send()
+    send(side, side, z_send.at[0], z_recv.at[0], partner).wait_send()
+    for n in range(2):
+        XB = (XB1, XB2)[n].at[0, :, :, pl.ds(0, (MODES, SIDE)[n])]
+        for up, present in ((1, has_high), (0, has_low)):
+            pl.when(present)(send(XB, XB, x_send.at[n, up], x_recv.at[n, up, 0], partner).wait_send)
     for n in range(2):
         _, yy = borders(n)
         pl.when(y_high)(yy(True).wait_send)
         pl.when(y_low)(yy(False).wait_send)
     pl.when(has_high)(a_copy(True).wait_send)
     pl.when(has_low)(a_copy(False).wait_send)
+    for n in range(2):
+        pltpu.make_async_copy(own, own, o_loc.at[n]).wait()
+        every = send(three, three, o_send.at[n], o_recv.at[n], partner)
+        every.wait_send()
+        every.wait_recv()
 
 
 def per_device(field, coeff, pairs, values):
@@ -480,23 +474,23 @@
             pltpu.VMEM((336, 256), F32),
             pltpu.VMEM((336, 256), BF16),
             pltpu.VMEM((192, 256), BF16),
-            sem((4, NC)),
-            sem((4, NC)),
-            sem((NC, 4)),
-            sem((NC, 4)),
+            sem((1,)),
+            sem((NC,)),
+            sem((1,)),
+            sem((NC,)),
             sem((2,)),
             sem((2,)),
-            sem((2, 2, NC)),
+            sem((2, 2)),
             sem((2, 2, NC)),
             sem((2, 2)),
             sem((2, 2)),
-            sem((2, 4, NC)),
-            sem((2, 4, NC)),
-            sem((3 + NC,)),
-            sem((2, NC)),
+            sem((2,)),
+            sem((2,)),
+            sem((4,)),
+            sem((2,)),
         ],
         compiler_params=pltpu.CompilerParams(
-            collective_id=0, has_side_effects=True, vmem_limit_bytes=48 << 20
+            collective_id=0, has_side_effects=True, vmem_limit_bytes=60 << 20
         ),
     )(
         field.reshape(OWN, LAYERS, 48, 1, 128),

time: 74.6 us -> 65.6 us (0.88)
  Pallas kernels: 68.4 us -> 61.8 us
  local copies, waits for them, and re-layouts: 5.26 us -> 2.91 us
    pallas_call x1, Pallas kernels: 68.4 us -> 61.8 us  [per_device(): pl.pallas_call(kernel, out_shape=(out, out), in_specs=[hbm, hbm, vmem, vm...]
    unnamed x10 -> x4, local copies, waits for them, and re-layouts: 5.26 us -> 2.91 us
where the time goes in v1:
time: 65.6 us; the launch traced here: 65.3 us
  Pallas kernels  61.8 us (94%)
  local copies, waits for them, and re-layouts  2.91 us (4%)
    pallas_call x1, Pallas kernels, per_device(): pl.pallas_call(kernel, out_shape=(out, out), in_specs=[hbm, hbm, vmem, vm...  61.8 us
    unnamed x4, local copies, waits for them, and re-layouts  2.91 us

profile of v1, /device:TPU:6, one launch (start us, length us, event | category | flops | bytes accessed | tf_op | source)
XLA Modules:
  0.0 65.3 jit_solution(1606998332562314496)
XLA Ops:
  0.6 61.8 %shard_map.59 = (f32[7,4,48,1,128]{4,3,2,1,0:T(1,128)}, f32[7,4,48,1,128]{4,3,2,1,0:T(1,128)}) custom-call(f32[7,4,48,1,128]{4,3,2,1,0:T(1,128)} %bitcast.5, f32[6,4,48,1,128]{4,3,2,1,0:T(1,128)} %bitcast.8, s32[6,2,168]{2,1,0:T(2,128)} %bitcast.9, f32[6,168]{1,0:T(8,128)} %values.1), custom_call_target="tpu_custom_call" | custom-call | tf_op jit(solution)/shard_map/pallas_call | solution.py:457
  62.4 0.0 copy-start
  62.4 2.1 %copy.8 = f32[7,4,48,128]{3,2,1,0:T(8,128)} copy(f32[7,4,48,128]{3,2,1,0:T(8,128)} %bitcast.7) | data formatting | bytes 1376256
  64.5 0.0 copy-done
  64.5 0.8 %copy.9 = f32[7,4,48,128]{3,2,1,0:T(8,128)} copy(f32[7,4,48,128]{3,2,1,0:T(8,128)S(1)} %bitcast.6) | data formatting | bytes 1376256
Async XLA Ops:
  62.4 2.1 %copy-start = (f32[7,4,48,1,128]{4,3,2,1,0:T(1,128)S(1)}, f32[7,4,48,1,128]{4,3,2,1,0:T(1,128)}, u32[]{:S(2)}) copy-start(f32[7,4,48,1,128]{4,3,2,1,0:T(1,128)} %get-tuple-element.5) | copy-start | bytes 2064388

commit v2 on v1

--- a/solution.py
+++ b/solution.py
@@ -20,10 +20,10 @@
 CELLS = LAYERS * ROWS
 FACES = 6
 HIGH_ROWS = ROWS + 2
-NR = 2
+NR = 1
 NC = ROWS // NR
-AHEAD = 3
-LAG = 2
+AHEAD = 5
+LAG = 4
 
 
 def kernel(
@@ -31,8 +31,7 @@
     coeff,
     pairs,
     values,
-    first_out,
-    second_out,
+    outs,
     U,
     F,
     S,
@@ -62,6 +61,7 @@
     loc,
     o_loc,
 ):
+    first_out, second_out = outs.at[0], outs.at[1]
     space = lax.axis_index("space")
     mode = lax.axis_index("mode")
     y = mode // 2
@@ -452,13 +452,13 @@
 def per_device(field, coeff, pairs, values):
     vmem = pl.BlockSpec(memory_space=pltpu.VMEM)
     hbm = pl.BlockSpec(memory_space=pl.ANY)
-    out = jax.ShapeDtypeStruct((OWN, LAYERS, 48, 1, 128), F32)
+    out = jax.ShapeDtypeStruct((2, OWN, LAYERS, 48, 1, 128), F32)
     sem = pltpu.SemaphoreType.DMA
-    first, second = pl.pallas_call(
+    both = pl.pallas_call(
         kernel,
-        out_shape=(out, out),
+        out_shape=out,
         in_specs=[hbm, hbm, vmem, vmem],
-        out_specs=(vmem, vmem),
+        out_specs=hbm,
         scratch_shapes=[
             pltpu.VMEM((NC, MODES, LAYERS, NR, 1, 128), F32),
             pltpu.VMEM((NC, MODES, LAYERS, NR, 1, 128), F32),
@@ -498,7 +498,7 @@
         jnp.transpose(pairs, (0, 2, 1)),
         values,
     )
-    return first.reshape(field.shape), second.reshape(field.shape)
+    return both[0].reshape(field.shape), both[1].reshape(field.shape)
 
 
 def solution(mesh):

time: 65.6 us -> 62.4 us (0.951)
  Pallas kernels: 61.8 us -> 59 us
    unnamed x4 -> x0, local copies, waits for them, and re-layouts: 2.91 us -> none
    pallas_call x1, Pallas kernels: 61.8 us -> 59 us  [per_device(): pl.pallas_call(kernel, out_shape=out, in_specs=[hbm, hbm, vmem, vmem], ou...]
    slice x0 -> x1, local copies, waits for them, and re-layouts: none -> 2.5 us  [per_device(): return (both[0].reshape(field.shape), both[1].reshape(field.shape))]
where the time goes in v2:
time: 62.4 us; the launch traced here: 62.2 us
  Pallas kernels  59 us (95%)
  local copies, waits for them, and re-layouts  2.5 us (4%)
  between operations  0.64 us (1%)
    pallas_call x1, Pallas kernels, per_device(): pl.pallas_call(kernel, out_shape=out, in_specs=[hbm, hbm, vmem, vmem], ou...  59 us
    slice x1, local copies, waits for them, and re-layouts, per_device(): return (both[0].reshape(field.shape), both[1].reshape(field.shape))  2.5 us

profile of v2, /device:TPU:6, one launch (start us, length us, event | category | flops | bytes accessed | tf_op | source)
XLA Modules:
  0.0 62.2 jit_solution(926895727420629265)
XLA Ops:
  0.6 59.0 %shard_map.59 = f32[2,7,4,48,1,128]{5,4,3,2,1,0:T(1,128)} custom-call(f32[7,4,48,1,128]{4,3,2,1,0:T(1,128)} %bitcast.5, f32[6,4,48,1,128]{4,3,2,1,0:T(1,128)} %bitcast.8, s32[6,2,168]{2,1,0:T(2,128)} %bitcast.9, f32[6,168]{1,0:T(8,128)} %values.1), custom_call_target="tpu_custom_call" | custom-call | tf_op jit(solution)/shard_map/pallas_call | solution.py:457
  59.7 2.5 %fusion = (f32[1,7,4,48,1,128]{5,4,3,2,1,0:T(1,128)}, f32[1,7,4,48,1,128]{5,4,3,2,1,0:T(1,128)}) fusion(f32[2,7,4,48,1,128]{5,4,3,2,1,0:T(1,128)} %shard_map.59), kind=kLoop, calls=%fused_computation | loop fusion | bytes 2752512 | tf_op jit(solution)/shard_map/slice | solution.py:501

commit v3 on v2

--- a/solution.py
+++ b/solution.py
@@ -23,6 +23,7 @@
 NR = 1
 NC = ROWS // NR
 AHEAD = 5
+AT_ONCE = 8
 LAG = 4
 
 
@@ -160,7 +161,10 @@
     def start_field(c):
         for step in (1, 3, 2):
             y_copy(step, c).start()
-        z_copy(c, 0).start()
+
+        @pl.when(c < AT_ONCE)
+        def _():
+            z_copy(c, 0).start()
 
     loop(NC, start_field)
 
@@ -197,6 +201,10 @@
     loop(NC, lambda c: own_copy(c).start())
 
     def y_to_z(c):
+        @pl.when(c >= AT_ONCE)
+        def _():
+            z_copy(c, 0).start()
+
         wait_y(c)
         for j in (1, 2, 3):
             z_copy(c, j).start()
@@ -498,7 +506,21 @@
         jnp.transpose(pairs, (0, 2, 1)),
         values,
     )
-    return both[0].reshape(field.shape), both[1].reshape(field.shape)
+    def place(x, a, b):
+        a[...] = x[0]
+        b[...] = x[1]
+
+    rows = OWN * LAYERS * 48
+    flat = jax.ShapeDtypeStruct((rows, 128), F32)
+    block = pl.BlockSpec((rows // 2, 128), lambda i: (i, 0))
+    first, second = pl.pallas_call(
+        place,
+        grid=(2,),
+        out_shape=(flat, flat),
+        in_specs=[pl.BlockSpec((2, rows // 2, 128), lambda i: (0, i, 0))],
+        out_specs=(block, block),
+    )(both.reshape(2, rows, 128))
+    return first.reshape(field.shape), second.reshape(field.shape)
 
 
 def solution(mesh):

time: 62.4 us -> 61.8 us (level)
  local copies, waits for them, and re-layouts: 2.5 us -> 0 us
  Pallas kernels: 59 us -> 60.4 us
    slice x1 -> x0, local copies, waits for them, and re-layouts: 2.5 us -> none  [per_device(): return (both[0].reshape(field.shape), both[1].reshape(field.shape))]
    pallas_call x0 -> x1, Pallas kernels: none -> 2.23 us  [per_device(): pl.pallas_call(place, grid=(2,), out_shape=(flat, flat), in_specs=[pl.Blo...]
    pallas_call x1, Pallas kernels: 59 us -> 58.1 us  [per_device(): pl.pallas_call(kernel, out_shape=out, in_specs=[hbm, hbm, vmem, vmem], ou...]
where the time goes in v3:
time: 61.8 us; the launch traced here: 61 us
  Pallas kernels  60.4 us (98%)
  between operations  0.64 us (1%)
    pallas_call x1, Pallas kernels, per_device(): pl.pallas_call(kernel, out_shape=out, in_specs=[hbm, hbm, vmem, vmem], ou...  58.1 us
    pallas_call x1, Pallas kernels, per_device(): pl.pallas_call(place, grid=(2,), out_shape=(flat, flat), in_specs=[pl.Blo...  2.23 us

profile of v3, /device:TPU:6, one launch (start us, length us, event | category | flops | bytes accessed | tf_op | source)
XLA Modules:
  0.0 61.0 jit_solution(9722137077570169473)
XLA Ops:
  0.6 58.1 %shard_map.59 = f32[2,7,4,48,1,128]{5,4,3,2,1,0:T(1,128)} custom-call(f32[7,4,48,1,128]{4,3,2,1,0:T(1,128)} %bitcast.7, f32[6,4,48,1,128]{4,3,2,1,0:T(1,128)} %bitcast.8, s32[6,2,168]{2,1,0:T(2,128)} %bitcast.9, f32[6,168]{1,0:T(8,128)} %values.1), custom_call_target="tpu_custom_call" | custom-call | tf_op jit(solution)/shard_map/pallas_call | solution.py:465
  58.8 2.2 %shard_map.60 = (f32[1344,128]{1,0:T(8,128)}, f32[1344,128]{1,0:T(8,128)}) custom-call(f32[2,1344,128]{2,1,0:T(8,128)} %bitcast.6), custom_call_target="tpu_custom_call" | custom-call | tf_op jit(solution)/shard_map/pallas_call | solution.py:516

commit v4 on v3

--- a/solution.py
+++ b/solution.py
@@ -104,8 +104,8 @@
     U2 = U.reshape(NC * MODES * LAYERS * NR, 128)
     F2 = F.reshape(NC * MODES * LAYERS * NR, 128)
     S2 = S.reshape(NC * 32 * LAYERS * NR, 128)
-    A2 = A.reshape(TERMS * 6 * HIGH_ROWS, 128)
-    FC2 = FC.reshape(CELLS * 36, 128)
+    A2 = A.reshape((TERMS + 1) * 6 * HIGH_ROWS, 128)
+    FC2 = FC.reshape((CELLS + 8) * 36, 128)
 
     A2[...] = jnp.zeros(A2.shape, F32)
 
@@ -169,16 +169,16 @@
     loop(NC, start_field)
 
     own_a = pltpu.make_async_copy(
-        coeff.at[:, :, pl.ds(y * ROWS, ROWS)], A.at[:, pl.ds(1, LAYERS), pl.ds(1, ROWS)], loc.at[0]
+        coeff.at[:, :, pl.ds(y * ROWS, ROWS)], A.at[pl.ds(0, TERMS), pl.ds(1, LAYERS), pl.ds(1, ROWS)], loc.at[0]
     )
     low_a = pltpu.make_async_copy(
         coeff.at[:, :, pl.ds(jnp.maximum(y * ROWS - 1, 0), 1)],
-        A.at[:, pl.ds(1, LAYERS), pl.ds(0, 1)],
+        A.at[pl.ds(0, TERMS), pl.ds(1, LAYERS), pl.ds(0, 1)],
         loc.at[1],
     )
     high_a = pltpu.make_async_copy(
         coeff.at[:, :, pl.ds(jnp.minimum(y * ROWS + ROWS, 47), 1)],
-        A.at[:, pl.ds(1, LAYERS), pl.ds(ROWS + 1, 1)],
+        A.at[pl.ds(0, TERMS), pl.ds(1, LAYERS), pl.ds(ROWS + 1, 1)],
         loc.at[2],
     )
 
@@ -186,7 +186,7 @@
         l, slot, s = (LAYERS - 1, 0, 1) if up else (0, LAYERS + 1, -1)
         return send(
             coeff.at[:, l, pl.ds(y * ROWS, ROWS)],
-            A.at[:, slot, pl.ds(1, ROWS)],
+            A.at[pl.ds(0, TERMS), slot, pl.ds(1, ROWS)],
             c_send.at[int(up)],
             c_recv.at[int(up)],
             near_peer(s),
@@ -475,8 +475,8 @@
             pltpu.VMEM((2, NC, NR, 32, 128), F32),
             pltpu.VMEM((2, LAYERS, MODES, 128), F32),
             pltpu.VMEM((2, LAYERS, 32, 128), F32),
-            pltpu.VMEM((TERMS, 6, HIGH_ROWS, 1, 128), F32),
-            pltpu.VMEM((CELLS * 36, 1, 128), F32),
+            pltpu.VMEM((TERMS + 1, 6, HIGH_ROWS, 1, 128), F32),
+            pltpu.VMEM(((CELLS + 8) * 36, 1, 128), F32),
             pltpu.VMEM((6, HIGH_ROWS, MODES, 128), F32),
             pltpu.VMEM((6, HIGH_ROWS, 32, 128), F32),
             pltpu.VMEM((336, 256), F32),

time: 61.8 us -> 61.8 us (level)
  no operation moved by 1% of the time
where the time goes in v4:
time: 61.8 us; the launch traced here: 61 us
  Pallas kernels  60.3 us (98%)
  between operations  0.64 us (1%)
    pallas_call x1, Pallas kernels, per_device(): pl.pallas_call(kernel, out_shape=out, in_specs=[hbm, hbm, vmem, vmem], ou...  58.1 us
    pallas_call x1, Pallas kernels, per_device(): pl.pallas_call(place, grid=(2,), out_shape=(flat, flat), in_specs=[pl.Blo...  2.23 us

profile of v4, /device:TPU:6, one launch (start us, length us, event | category | flops | bytes accessed | tf_op | source)
XLA Modules:
  0.0 61.0 jit_solution(2011355287287361812)
XLA Ops:
  0.6 58.1 %shard_map.59 = f32[2,7,4,48,1,128]{5,4,3,2,1,0:T(1,128)} custom-call(f32[7,4,48,1,128]{4,3,2,1,0:T(1,128)} %bitcast.7, f32[6,4,48,1,128]{4,3,2,1,0:T(1,128)} %bitcast.8, s32[6,2,168]{2,1,0:T(2,128)} %bitcast.9, f32[6,168]{1,0:T(8,128)} %values.1), custom_call_target="tpu_custom_call" | custom-call | tf_op jit(solution)/shard_map/pallas_call | solution.py:465
  58.7 2.2 %shard_map.60 = (f32[1344,128]{1,0:T(8,128)}, f32[1344,128]{1,0:T(8,128)}) custom-call(f32[2,1344,128]{2,1,0:T(8,128)} %bitcast.6), custom_call_target="tpu_custom_call" | custom-call | tf_op jit(solution)/shard_map/pallas_call | solution.py:516

commit v5 on v4

--- a/solution.py
+++ b/solution.py
@@ -159,7 +159,7 @@
         return pltpu.make_async_copy(own_rows(c), U.at[c, pl.ds(zhi * SIDE + y * OWN, OWN)], loc.at[3])
 
     def start_field(c):
-        for step in (1, 3, 2):
+        for step in (2, 1, 3):
             y_copy(step, c).start()
 
         @pl.when(c < AT_ONCE)

time: 61.8 us -> 61.7 us (level)
  no operation moved by 1% of the time
where the time goes in v5:
time: 61.7 us; the launch traced here: 61 us
  Pallas kernels  60.4 us (98%)
  between operations  0.64 us (1%)
    pallas_call x1, Pallas kernels, per_device(): pl.pallas_call(kernel, out_shape=out, in_specs=[hbm, hbm, vmem, vmem], ou...  58.1 us
    pallas_call x1, Pallas kernels, per_device(): pl.pallas_call(place, grid=(2,), out_shape=(flat, flat), in_specs=[pl.Blo...  2.23 us

profile of v5, /device:TPU:6, one launch (start us, length us, event | category | flops | bytes accessed | tf_op | source)
XLA Modules:
  0.0 61.0 jit_solution(14111128646568224175)
XLA Ops:
  0.6 58.1 %shard_map.59 = f32[2,7,4,48,1,128]{5,4,3,2,1,0:T(1,128)} custom-call(f32[7,4,48,1,128]{4,3,2,1,0:T(1,128)} %bitcast.7, f32[6,4,48,1,128]{4,3,2,1,0:T(1,128)} %bitcast.8, s32[6,2,168]{2,1,0:T(2,128)} %bitcast.9, f32[6,168]{1,0:T(8,128)} %values.1), custom_call_target="tpu_custom_call" | custom-call | tf_op jit(solution)/shard_map/pallas_call | solution.py:465
  58.8 2.2 %shard_map.60 = (f32[1344,128]{1,0:T(8,128)}, f32[1344,128]{1,0:T(8,128)}) custom-call(f32[2,1344,128]{2,1,0:T(8,128)} %bitcast.6), custom_call_target="tpu_custom_call" | custom-call | tf_op jit(solution)/shard_map/pallas_call | solution.py:516
